TPU v7x, 512 devices: a whole 4x4x16 slice. The times are simulated.
512 devices in a mesh: lev: 4 (over y), lat: 4 (over x), lon: 32 (over z, core).
Axes of the slice: x: 4, y: 4, z: 16, core: 2. Of those that a mesh axis runs over, the one named last changes fastest.
Arguments:
- anomalies: bfloat16 [64, 512, 2560], P('lat', 'lon', 'lev'), may hold values from -6 to 6
- error_grad: float32 [64, 512, 32], P('lat', 'lon', 'lev'), may hold values from -288 to 288
- obs_lat: float32 [4, 32, 2048], P('lat', 'lon'), may hold values from 0 to 16
- obs_lon: float32 [4, 32, 2048], P('lat', 'lon'), may hold values from 0 to 16
- obs_level: int32 [4, 32, 2048], P('lat', 'lon'), may hold values from 0 to 31
- obs_count: int32 [4, 32], P('lat', 'lon'), may hold values from 512 to 2048, as said below
- obs_pert: bfloat16 [4, 32, 80, 2048], P('lat', 'lon'), may hold values from -6 to 6
- innovation: float32 [4, 32, 2048], P('lat', 'lon'), may hold values from -6 to 6
- inv_error: float32 [4, 32, 2048], P('lat', 'lon'), may hold values from 0.25 to 4
Outputs:
- impact: float32 [4, 32, 2048], P('lat', 'lon')
Inputs may be any that keep to these rules, and one draw needn't show every extreme that they name: Live observations occupy the first obs_count slots of a tile's block; entries of other slots are arbitrary. Exactly one tile holds 2048 observations; the others hold from 512 to 1280.
All inputs are finite; a program needn't handle non-finite values.
Results may differ from a plain program's by a relative error of at most 0.0041.
Values may be sent and summed in bfloat16 or wider, within the bound.
A program may use at most 64 MiB of HBM per device.

v0:
```python
import functools

import jax
import jax.numpy as jnp
from jax import lax
from jax.experimental import pallas as pl
from jax.experimental.pallas import tpu as pltpu
from jax.sharding import PartitionSpec as P

MESH = pl.DeviceIdType.MESH
LANES = 128
HALF = 8
QUAD = HALF * HALF
OWN, BAND, RIGHT, LEFT = range(4)


def vertical_taper(dist, support):
    r = 2.0 * dist / support
    inner = (((-0.25 * r + 0.5) * r + 0.625) * r - 5.0 / 3.0) * r * r + 1.0
    safe_r = jnp.maximum(r, 1.0)
    outer = (
        ((((r / 12.0 - 0.5) * r + 0.625) * r + 5.0 / 3.0) * r - 5.0) * r
        + 4.0
        - 2.0 / (3.0 * safe_r)
    )
    return jnp.where(r <= 1.0, inner, jnp.where(r < 2.0, outer, 0.0))


def taper_of_square(q):
    s = lax.rsqrt(q)
    r = q * s
    inner = 1.0 + q * (0.5 * q - 5.0 / 3.0) + (q * r) * (0.625 - 0.25 * q)
    t = jnp.maximum(2.0 - r, 0.0)
    t = t * t
    outer = (t * t) * ((r + 2.0) * (1.0 / 12.0) - s * (1.0 / 24.0))
    return jnp.where(r <= 1.0, inner, outer)


def wrapped(i, n):
    return lax.rem(i + n, n)


def kernel(
    sizes,
    anomalies_in,
    error_grad_in,
    obs_lat_in,
    obs_lon_in,
    obs_level_in,
    obs_count_in,
    obs_pert_in,
    innovation_in,
    inv_error_in,
    impact,
    anomalies,
    error_grad,
    obs_lat,
    obs_lon,
    obs_level,
    obs_count,
    obs_pert,
    innovation,
    inv_error,
    cells,
    terms,
    rho,
    total,
    parts,
    in_sem,
    send_sem,
    recv_sem,
    lev_send,
    lev_recv,
    left_in,
):
    levs, lats, lons = sizes
    rows, depth, cols = error_grad.shape
    width = cells.shape[3]
    members = width // depth
    slots = terms.shape[1]
    tile = min(256, slots)
    lev, lat, lon = (lax.axis_index(a) for a in ("lev", "lat", "lon"))
    below, above = wrapped(lat + 1, lats), wrapped(lat - 1, lats)
    right, left = wrapped(lon + 1, lons), wrapped(lon - 1, lons)

    loads = [
        pltpu.make_async_copy(src, dst, in_sem.at[n])
        for n, (src, dst) in enumerate(
            (
                (error_grad_in, error_grad),
                (anomalies_in, anomalies),
                (obs_level_in, obs_level),
                (obs_count_in, obs_count),
                (obs_pert_in, obs_pert),
                (obs_lat_in, obs_lat),
                (obs_lon_in, obs_lon),
                (innovation_in, innovation),
                (inv_error_in, inv_error),
            )
        )
    ]
    for load in loads:
        load.start()

    has_above, has_below = lat > 0, lat < lats - 1

    def guarded(wanted, act):
        if wanted is None:
            act()
        else:
            pl.when(wanted)(act)

    def signal(sem, other, wanted=None):
        guarded(
            wanted,
            lambda: pl.semaphore_signal(sem, inc=1, device_id=other, device_id_type=MESH),
        )

    barrier = pltpu.get_barrier_semaphore()
    signal(barrier, {"lon": left})
    for k in range(1, levs):
        signal(barrier, {"lev": wrapped(lev + k, levs)})
    for other, wanted in ((above, has_above), (below, has_below)):
        signal(barrier, {"lat": other, "lon": left}, wanted)
        signal(barrier, {"lat": other}, wanted)
    beside = has_above.astype(jnp.int32) + has_below.astype(jnp.int32)

    pairs = rows * depth
    level_of = lax.broadcasted_iota(jnp.int32, (pairs, width), 0) % depth * members
    lane = lax.broadcasted_iota(jnp.int32, (pairs, width), 1)
    inside = jnp.logical_and(lane >= level_of, lane < level_of + members)
    ones = jnp.where(inside, 1.0, 0.0).astype(jnp.bfloat16)
    ones = jnp.concatenate([ones] * 3, axis=0)
    row_of = lax.broadcasted_iota(jnp.int32, (HALF, pairs), 1) // depth
    loads[0].wait()
    rest = error_grad[...].reshape(pairs, cols).T
    grads = []
    for _ in range(3):
        grads.append(rest.astype(jnp.bfloat16).astype(jnp.float32))
        rest = rest - grads[-1]

    def weigh(qx):
        half = slice(qx * HALF, (qx + 1) * HALF)
        wide = [
            jnp.concatenate([jnp.where(row_of == y, grad[half], 0.0) for y in range(rows)], axis=0)
            for grad in grads
        ]
        wide = jnp.concatenate(wide, axis=1).astype(jnp.bfloat16)
        spread = jnp.dot(wide, ones, preferred_element_type=jnp.float32)
        for y in range(0, rows, 2):
            both = [anomalies[n].astype(jnp.float32)[half] for n in (y, y + 1)]
            both = jnp.concatenate(both, axis=0) * spread[y * HALF : (y + 2) * HALF]
            at = y % HALF * HALF
            cells[OWN, qx * 2 + y // HALF, at : at + 2 * HALF] = both.astype(jnp.bfloat16)

    class Copy:
        def __init__(self, sem, quads, piece, place, device, sends=None, gets=None):
            self.sends, self.gets = sends, gets
            self.copy = pltpu.make_async_remote_copy(
                src_ref=cells.at[OWN, quads],
                dst_ref=cells.at[piece, place],
                send_sem=send_sem.at[sem],
                recv_sem=recv_sem.at[sem],
                device_id=device,
                device_id_type=MESH,
            )

        def start(self):
            guarded(self.sends, self.copy.start)

        def wait_recv(self):
            guarded(self.gets, self.copy.wait_recv)

        def wait_send(self):
            guarded(self.sends, self.copy.wait_send)

    down, up = (has_below, has_above), (has_above, has_below)
    to_right = [
        Copy(1, 3, LEFT, 2, {"lat": below, "lon": right}, *down),
        Copy(2, 2, LEFT, 3, {"lat": above, "lon": right}, *up),
        Copy(0, pl.ds(2, 2), LEFT, pl.ds(0, 2), {"lon": right}),
    ]
    to_left = [
        Copy(4, 1, RIGHT, 2, {"lat": below, "lon": left}, *down),
        Copy(5, 0, RIGHT, 3, {"lat": above, "lon": left}, *up),
        Copy(3, pl.ds(0, 2), RIGHT, pl.ds(0, 2), {"lon": left}),
    ]
    to_bands = [
        Copy(6, 1, BAND, 0, {"lat": below}, *down),
        Copy(7, 3, BAND, 1, {"lat": below}, *down),
        Copy(8, 0, BAND, 2, {"lat": above}, *up),
        Copy(9, 2, BAND, 3, {"lat": above}, *up),
    ]

    loads[1].wait()
    weigh(1)
    pl.semaphore_wait(barrier, levs + 2 * beside)
    for send in to_right:
        send.start()
    signal(left_in, {"lon": right})
    for other, wanted in ((above, has_above), (below, has_below)):
        signal(left_in, {"lat": other, "lon": right}, wanted)
    weigh(0)
    for send in to_bands:
        send.start()

    for load in loads[2:7]:
        load.wait()

    def make_terms(n, carry):
        at = pl.ds(pl.multiple_of(n * tile, tile), tile)
        level = lax.broadcasted_iota(jnp.int32, (depth, tile), 0) + lev * depth
        slot = lax.broadcasted_iota(jnp.int32, (depth, tile), 1) + n * tile
        away = jnp.abs(obs_level[:, at] - level).astype(jnp.float32)
        live = (slot < obs_count[0, 0]).astype(jnp.float32)
        vertical = vertical_taper(away, depth) * live
        pert = obs_pert[:, at].astype(jnp.float32)
        for m in range(depth):
            terms[m * members : (m + 1) * members, at] = (pert * vertical[m : m + 1]).astype(
                jnp.bfloat16
            )
        return carry

    lax.fori_loop(0, slots // tile, make_terms, 0)

    def offset_x(at, side):
        centre = (lax.broadcasted_iota(jnp.int32, (HALF, tile), 0) + side * HALF).astype(jnp.float32)
        return (obs_lon[:, at] - (centre + (0.5 - HALF))) * (2.0 / HALF)

    def make_rho(n, carry):
        at = pl.ds(pl.multiple_of(n * tile, tile), tile)
        squares = []
        for side in range(2):
            dx = offset_x(at, side)
            dx = jnp.where(dx < 2.0, dx, dx - 4.0)
            squares.append(dx * dx + 1e-30)
        for j in range(2 * HALF):
            dy = (obs_lat[:, at] - (j + 0.5 - HALF)) * (2.0 / HALF)
            near = dy < 2.0
            dy = jnp.where(near, dy, dy - 4.0)
            dy2 = jnp.broadcast_to(dy * dy, (HALF, tile))
            near = jnp.broadcast_to(jnp.where(near, 1.0, 0.0), (HALF, tile)) > 0.5
            for side in range(2):
                value = taper_of_square(dy2 + squares[side])
                cols = slice(side * HALF, (side + 1) * HALF)
                rho[0, j, cols, at] = jnp.where(near, value, 0.0)
                rho[1, j, cols, at] = jnp.where(near, 0.0, value)
        return carry

    lax.fori_loop(0, slots // tile, make_rho, 0)

    def send_left():
        pl.semaphore_wait(left_in, 1 + beside)
        for send in to_left:
            send.start()

    @pl.when(lon > 0)
    def _():
        send_left()

    total[...] = jnp.zeros_like(total)

    def add_piece(piece, start, quads):
        for n in range(slots // tile):
            at = slice(n * tile, (n + 1) * tile)
            near = [offset_x(at, side) < 2.0 for side in range(2)]
            weights = cells[piece, start : start + len(quads)].reshape(len(quads) * QUAD, width)
            both = jnp.dot(weights, terms[:, at], preferred_element_type=jnp.float32)
            acc = total[:, at]
            for n_quad, (row, col) in enumerate(quads):
                a, j, b, i = row // 2, row % 2, col // 2, col % 2
                part = both[n_quad * QUAD : (n_quad + 1) * QUAD].reshape(HALF, HALF, tile)
                part = part * rho[a, j * HALF : (j + 1) * HALF, i * HALF : (i + 1) * HALF, at]
                part = jnp.sum(part, axis=0)
                keep = near[i] if b == 0 else jnp.logical_not(near[i])
                if row == 0:
                    keep = jnp.logical_and(keep, lat > 0)
                elif row == 3:
                    keep = jnp.logical_and(keep, lat < lats - 1)
                acc = acc + jnp.where(keep, part, 0.0)
            total[:, at] = acc

    add_piece(OWN, 0, [(1, 1), (2, 1), (1, 2), (2, 2)])

    for send in to_bands:
        send.wait_recv()
    add_piece(BAND, 0, [(0, 1), (0, 2), (3, 1), (3, 2)])
    @pl.when(lon == 0)
    def _():
        send_left()

    for send in to_left:
        send.wait_recv()
    add_piece(RIGHT, 0, [(1, 3), (2, 3), (0, 3), (3, 3)])
    for send in to_right[:2]:
        send.wait_recv()
    add_piece(LEFT, 2, [(0, 0), (3, 0)])
    to_right[2].wait_recv()
    add_piece(LEFT, 0, [(1, 0), (2, 0)])

    parts[lev] = jnp.sum(total[...], axis=0, keepdims=True)
    swaps = []
    for k in range(1, levs):
        swaps.append(
            pltpu.make_async_remote_copy(
                src_ref=parts.at[lev],
                dst_ref=parts.at[lev],
                send_sem=lev_send.at[k - 1],
                recv_sem=lev_recv.at[k - 1],
                device_id={"lev": wrapped(lev + k, levs)},
                device_id_type=MESH,
            )
        )
        swaps[-1].start()
    for swap in swaps:
        swap.wait_recv()
    value = parts[0]
    for k in range(1, levs):
        value = value + parts[k]
    for load in loads[7:]:
        load.wait()
    impact[...] = innovation[...] * inv_error[...] * value / (members - 1.0)

    for send in swaps + to_right + to_bands + to_left:
        send.wait_send()


def per_device(
    sizes,
    anomalies,
    error_grad,
    obs_lat,
    obs_lon,
    obs_level,
    obs_count,
    obs_pert,
    innovation,
    inv_error,
):
    rows, cols, width = anomalies.shape
    depth = error_grad.shape[2]
    members, slots = obs_pert.shape[2:]
    in_specs = [pl.BlockSpec(memory_space=pltpu.HBM)] * 9
    flat = (1, slots)
    impact = pl.pallas_call(
        functools.partial(kernel, sizes),
        out_shape=pltpu.VMEM(flat, jnp.float32),
        in_specs=in_specs,
        out_specs=pl.BlockSpec(memory_space=pltpu.VMEM),
        scratch_shapes=[
            pltpu.VMEM((rows, cols, width), jnp.bfloat16),
            pltpu.VMEM((rows, depth, cols), jnp.float32),
            pltpu.VMEM(flat, jnp.float32),
            pltpu.VMEM(flat, jnp.float32),
            pltpu.VMEM(flat, jnp.int32),
            pltpu.SMEM((1, 1), jnp.int32),
            pltpu.VMEM((members, slots), jnp.bfloat16),
            pltpu.VMEM(flat, jnp.float32),
            pltpu.VMEM(flat, jnp.float32),
            pltpu.VMEM((4, 4, QUAD, width), jnp.bfloat16),
            pltpu.VMEM((width, slots), jnp.bfloat16),
            pltpu.VMEM((2, rows, cols, slots), jnp.float32),
            pltpu.VMEM((HALF, slots), jnp.float32),
            pltpu.VMEM((sizes[0], 1, slots), jnp.float32),
            pltpu.SemaphoreType.DMA((9,)),
            pltpu.SemaphoreType.DMA((10,)),
            pltpu.SemaphoreType.DMA((10,)),
            pltpu.SemaphoreType.DMA((sizes[0] - 1,)),
            pltpu.SemaphoreType.DMA((sizes[0] - 1,)),
            pltpu.SemaphoreType.REGULAR,
        ],
        compiler_params=pltpu.CompilerParams(
            collective_id=0, has_side_effects=True, vmem_limit_bytes=58 * 1024 * 1024
        ),
        cost_estimate=pl.CostEstimate(
            flops=2 * 4 * rows * cols * width * slots, bytes_accessed=4 * 10**6, transcendentals=0
        ),
    )(
        anomalies,
        error_grad.transpose(0, 2, 1),
        obs_lat.reshape(flat),
        obs_lon.reshape(flat),
        obs_level.reshape(flat),
        obs_count,
        obs_pert.reshape(members, slots),
        innovation.reshape(flat),
        inv_error.reshape(flat),
    )
    return impact.reshape(1, 1, slots)


def solution(mesh):
    sizes = tuple(mesh.shape[a] for a in ("lev", "lat", "lon"))
    tiles = P("lat", "lon", None)
    placed = (
        P("lat", "lon", "lev"),
        P("lat", "lon", "lev"),
        tiles,
        tiles,
        tiles,
        P("lat", "lon"),
        P("lat", "lon", None, None),
        tiles,
        tiles,
    )
    return jax.shard_map(
        functools.partial(per_device, sizes),
        mesh=mesh,
        in_specs=placed,
        out_specs=tiles,
        check_vma=False,
    )
```

profile of v0, /device:TPU:2, one launch (start us, length us, event | category | flops | bytes accessed | tf_op | source)
XLA Modules:
  0.0 23.3 jit_solution(5031637379021713422)
XLA Ops:
  0.7 22.0 %shard_map.91 = f32[1,2048]{1,0:T(1,128)S(1)} custom-call(bf16[16,16,640]{2,1,0:T(8,128)(2,1)} %anomalies_in.1, f32[16,8,16]{2,1,0:T(8,128)} %bitcast.10, f32[1,2048]{1,0:T(1,128)} %bitcast.11, f32[1,2048]{1,0:T(1,128)} %bitcast.12, s32[1,2048]{1,0:T(1,128)} %bitcast.13, s32[1,1]{1,0:T(1,128)S(6)} %copy.12.obs_count_in, bf16[80,2048]{1,0:T(8,128)(2,1)} %bitcast.9, ...), custom_call_target="tpu_custom_call" | custom-call | flops 2684354560 | bytes 4000000 | tf_op jit(solution)/shard_map/pallas_call | solution.py:345
  22.7 0.6 %copy.11 = f32[1,1,2048]{2,1,0:T(1,128)} copy(f32[1,1,2048]{2,1,0:T(1,128)S(1)} %bitcast.8) | data formatting | bytes 16384
where the time goes:
time: 23.4 us; the launch traced here: 23.3 us
  Pallas kernels  22 us (94%)
  between operations  0.66 us (3%)
  local copies, waits for them, and re-layouts  0.6 us (3%)
    pallas_call x1, Pallas kernels, per_device(): pl.pallas_call(functools.partial(kernel, sizes), out_shape=pltpu.VMEM(fla...  22 us
    unnamed x1, local copies, waits for them, and re-layouts  0.6 us

commit v1 on v0

--- a/solution.py
+++ b/solution.py
@@ -72,6 +72,8 @@
     lev_send,
     lev_recv,
     left_in,
+    levs_in,
+    strip_sem,
 ):
     levs, lats, lons = sizes
     rows, depth, cols = error_grad.shape
@@ -88,7 +90,6 @@
         for n, (src, dst) in enumerate(
             (
                 (error_grad_in, error_grad),
-                (anomalies_in, anomalies),
                 (obs_level_in, obs_level),
                 (obs_count_in, obs_count),
                 (obs_pert_in, obs_pert),
@@ -99,7 +100,16 @@
             )
         )
     ]
-    for load in loads:
+    share = rows // 4
+    strips = [
+        pltpu.make_async_copy(
+            anomalies_in.at[pl.ds(n * share, share)],
+            anomalies.at[pl.ds(n * share, share)],
+            strip_sem.at[n],
+        )
+        for n in range(4)
+    ]
+    for load in [loads[0], *strips[2:], *strips[:2]]:
         load.start()
 
     has_above, has_below = lat > 0, lat < lats - 1
@@ -116,13 +126,17 @@
             lambda: pl.semaphore_signal(sem, inc=1, device_id=other, device_id_type=MESH),
         )
 
+    inner = lon < lons - 1
+    leads = lev == 0
     barrier = pltpu.get_barrier_semaphore()
+    signal(barrier, {"lev": 0}, jnp.logical_not(leads))
+    for other, wanted in ((above, has_above), (below, has_below)):
+        signal(barrier, {"lat": other}, jnp.logical_and(wanted, inner))
+
     signal(barrier, {"lon": left})
-    for k in range(1, levs):
-        signal(barrier, {"lev": wrapped(lev + k, levs)})
     for other, wanted in ((above, has_above), (below, has_below)):
         signal(barrier, {"lat": other, "lon": left}, wanted)
-        signal(barrier, {"lat": other}, wanted)
+
     beside = has_above.astype(jnp.int32) + has_below.astype(jnp.int32)
 
     pairs = rows * depth
@@ -139,26 +153,31 @@
         grads.append(rest.astype(jnp.bfloat16).astype(jnp.float32))
         rest = rest - grads[-1]
 
-    def weigh(qx):
+    def spread_over(qx):
         half = slice(qx * HALF, (qx + 1) * HALF)
         wide = [
             jnp.concatenate([jnp.where(row_of == y, grad[half], 0.0) for y in range(rows)], axis=0)
             for grad in grads
         ]
         wide = jnp.concatenate(wide, axis=1).astype(jnp.bfloat16)
-        spread = jnp.dot(wide, ones, preferred_element_type=jnp.float32)
-        for y in range(0, rows, 2):
+        return jnp.dot(wide, ones, preferred_element_type=jnp.float32)
+
+    def weigh(qx, qy, spread):
+        half = slice(qx * HALF, (qx + 1) * HALF)
+        for y in range(qy * HALF, (qy + 1) * HALF, 2):
             both = [anomalies[n].astype(jnp.float32)[half] for n in (y, y + 1)]
             both = jnp.concatenate(both, axis=0) * spread[y * HALF : (y + 2) * HALF]
             at = y % HALF * HALF
             cells[OWN, qx * 2 + y // HALF, at : at + 2 * HALF] = both.astype(jnp.bfloat16)
 
     class Copy:
-        def __init__(self, sem, quads, piece, place, device, sends=None, gets=None):
+        def __init__(
+            self, sem, quads, piece, place, device, sends=None, gets=None, part=slice(None)
+        ):
             self.sends, self.gets = sends, gets
             self.copy = pltpu.make_async_remote_copy(
-                src_ref=cells.at[OWN, quads],
-                dst_ref=cells.at[piece, place],
+                src_ref=cells.at[OWN, quads, :, part],
+                dst_ref=cells.at[piece, place, :, part],
                 send_sem=send_sem.at[sem],
                 recv_sem=recv_sem.at[sem],
                 device_id=device,
@@ -178,7 +197,12 @@
     to_right = [
         Copy(1, 3, LEFT, 2, {"lat": below, "lon": right}, *down),
         Copy(2, 2, LEFT, 3, {"lat": above, "lon": right}, *up),
-        Copy(0, pl.ds(2, 2), LEFT, pl.ds(0, 2), {"lon": right}),
+    ]
+    cut = width * 4 // 5 // LANES * LANES
+    spans = [slice(0, cut), slice(cut, width)]
+    to_right += [
+        Copy(sem, pl.ds(2, 2), LEFT, pl.ds(0, 2), {"lon": right}, part=span)
+        for sem, span in zip((0, 10), spans)
     ]
     to_left = [
         Copy(4, 1, RIGHT, 2, {"lat": below, "lon": left}, *down),
@@ -192,19 +216,40 @@
         Copy(9, 2, BAND, 3, {"lat": above}, *up),
     ]
 
-    loads[1].wait()
-    weigh(1)
-    pl.semaphore_wait(barrier, levs + 2 * beside)
-    for send in to_right:
+    spread = spread_over(1)
+    for strip in strips[2:]:
+        strip.wait()
+    weigh(1, 1, spread)
+    bands_in = jnp.where(inner, beside, 0)
+    pl.semaphore_wait(barrier, 1 + beside + bands_in + jnp.where(leads, levs - 1, 0))
+    to_right[0].start()
+    for strip in strips[:2]:
+        strip.wait()
+    weigh(1, 0, spread)
+    for send in to_right[1:]:
         send.start()
+    for load in loads[1:]:
+        load.start()
+
+    @pl.when(leads)
+    def _():
+        for k in range(1, levs):
+            signal(levs_in, {"lev": k})
+
     signal(left_in, {"lon": right})
     for other, wanted in ((above, has_above), (below, has_below)):
         signal(left_in, {"lat": other, "lon": right}, wanted)
-    weigh(0)
-    for send in to_bands:
-        send.start()
-
-    for load in loads[2:7]:
+    spread = spread_over(0)
+    for qy in range(2):
+        weigh(0, qy, spread)
+
+    def send_bands():
+        for send in to_bands:
+            send.start()
+
+    pl.when(inner)(send_bands)
+
+    for load in loads[1:6]:
         load.wait()
 
     def make_terms(n, carry):
@@ -258,14 +303,16 @@
     def _():
         send_left()
 
+    pl.when(jnp.logical_not(inner))(send_bands)
+
     total[...] = jnp.zeros_like(total)
 
-    def add_piece(piece, start, quads):
+    def add_piece(piece, start, quads, span=slice(None)):
         for n in range(slots // tile):
             at = slice(n * tile, (n + 1) * tile)
             near = [offset_x(at, side) < 2.0 for side in range(2)]
-            weights = cells[piece, start : start + len(quads)].reshape(len(quads) * QUAD, width)
-            both = jnp.dot(weights, terms[:, at], preferred_element_type=jnp.float32)
+            weights = cells[piece, start : start + len(quads), :, span].reshape(len(quads) * QUAD, -1)
+            both = jnp.dot(weights, terms[span, at], preferred_element_type=jnp.float32)
             acc = total[:, at]
             for n_quad, (row, col) in enumerate(quads):
                 a, j, b, i = row // 2, row % 2, col // 2, col % 2
@@ -285,18 +332,24 @@
     for send in to_bands:
         send.wait_recv()
     add_piece(BAND, 0, [(0, 1), (0, 2), (3, 1), (3, 2)])
+    for send in to_left:
+        send.wait_recv()
+    add_piece(RIGHT, 0, [(1, 3), (2, 3), (0, 3), (3, 3)])
+
     @pl.when(lon == 0)
     def _():
         send_left()
 
-    for send in to_left:
-        send.wait_recv()
-    add_piece(RIGHT, 0, [(1, 3), (2, 3), (0, 3), (3, 3)])
     for send in to_right[:2]:
         send.wait_recv()
     add_piece(LEFT, 2, [(0, 0), (3, 0)])
-    to_right[2].wait_recv()
-    add_piece(LEFT, 0, [(1, 0), (2, 0)])
+    for send, span in zip(to_right[2:], spans):
+        send.wait_recv()
+        add_piece(LEFT, 0, [(1, 0), (2, 0)], span)
+
+    @pl.when(jnp.logical_not(leads))
+    def _():
+        pl.semaphore_wait(levs_in, 1)
 
     parts[lev] = jnp.sum(total[...], axis=0, keepdims=True)
     swaps = []
@@ -317,7 +370,7 @@
     value = parts[0]
     for k in range(1, levs):
         value = value + parts[k]
-    for load in loads[7:]:
+    for load in loads[6:]:
         load.wait()
     impact[...] = innovation[...] * inv_error[...] * value / (members - 1.0)
 
@@ -363,11 +416,13 @@
             pltpu.VMEM((HALF, slots), jnp.float32),
             pltpu.VMEM((sizes[0], 1, slots), jnp.float32),
             pltpu.SemaphoreType.DMA((9,)),
-            pltpu.SemaphoreType.DMA((10,)),
-            pltpu.SemaphoreType.DMA((10,)),
+            pltpu.SemaphoreType.DMA((11,)),
+            pltpu.SemaphoreType.DMA((11,)),
             pltpu.SemaphoreType.DMA((sizes[0] - 1,)),
             pltpu.SemaphoreType.DMA((sizes[0] - 1,)),
             pltpu.SemaphoreType.REGULAR,
+            pltpu.SemaphoreType.REGULAR,
+            pltpu.SemaphoreType.DMA((4,)),
         ],
         compiler_params=pltpu.CompilerParams(
             collective_id=0, has_side_effects=True, vmem_limit_bytes=58 * 1024 * 1024

time: 23.4 us -> 23 us (0.983)
  Pallas kernels: 22 us -> 21.5 us
    pallas_call x1, Pallas kernels: 22 us -> 21.5 us  [per_device(): pl.pallas_call(functools.partial(kernel, sizes), out_shape=pltpu.VMEM(fla...]
where the time goes in v1:
time: 23 us; the launch traced here: 22.8 us
  Pallas kernels  21.5 us (93%)
  between operations  0.66 us (3%)
  local copies, waits for them, and re-layouts  0.6 us (3%)
    pallas_call x1, Pallas kernels, per_device(): pl.pallas_call(functools.partial(kernel, sizes), out_shape=pltpu.VMEM(fla...  21.5 us
    unnamed x1, local copies, waits for them, and re-layouts  0.6 us

profile of v1, /device:TPU:2, one launch (start us, length us, event | category | flops | bytes accessed | tf_op | source)
XLA Modules:
  0.0 22.8 jit_solution(5779560543066125274)
XLA Ops:
  0.7 21.5 %shard_map.91 = f32[1,2048]{1,0:T(1,128)S(1)} custom-call(bf16[16,16,640]{2,1,0:T(8,128)(2,1)} %anomalies_in.1, f32[16,8,16]{2,1,0:T(8,128)} %bitcast.10, f32[1,2048]{1,0:T(1,128)} %bitcast.11, f32[1,2048]{1,0:T(1,128)} %bitcast.12, s32[1,2048]{1,0:T(1,128)} %bitcast.13, s32[1,1]{1,0:T(1,128)S(6)} %copy.12.obs_count_in, bf16[80,2048]{1,0:T(8,128)(2,1)} %bitcast.9, ...), custom_call_target="tpu_custom_call" | custom-call | flops 2684354560 | bytes 4000000 | tf_op jit(solution)/shard_map/pallas_call | solution.py:398
  22.2 0.6 %copy.11 = f32[1,1,2048]{2,1,0:T(1,128)} copy(f32[1,1,2048]{2,1,0:T(1,128)S(1)} %bitcast.8) | data formatting | bytes 16384
